TPU v7x, 256 devices: a whole 4x4x8 slice. The times are simulated.
256 devices in a mesh: px: 32 (over z_lo, y, core), py: 8 (over x, z_hi).
Axes of the slice: x: 4, y: 4, z: 8 (z_hi: 2, z_lo: 4; z = z_hi * 4 + z_lo), core: 2. Of those that a mesh axis runs over, the one named last changes fastest.
Arguments:
- nodal_field: float32 [32, 8, 4096], P('px', 'py'), may hold values from -6 to 6
- element_matrix: float32 [32, 8, 16, 16384], P('px', 'py'), may hold values from -0.75 to 0.75
- connectivity: int32 [32, 8, 4, 16384], P('px', 'py'), may hold values from 0 to 4079
- face_nodes: int32 [32, 8, 4, 256], P('px', 'py'), may hold values from 0 to 4095, as said below
- panel_node: int32 [32, 8, 512], P('px', 'py'), may hold values from 0 to 4095
- panel_weight: float32 [32, 8, 512], P('px', 'py'), may hold values from 0.02 to 0.08
- centroid: float32 [32, 8, 3, 512], P('px', 'py'), may hold values from -1 to 1
- panel_normal: float32 [32, 8, 3, 512], P('px', 'py'), may hold values from -1 to 1, as said below
- panel_count: int32 [32, 8], replicated, may hold values from 256 to 512, as said below
- target_index: int32 [32, 8, 256], P('px', 'py'), may hold values from 0 to 255
- round_owner: int32 [8], replicated, may hold values from 0 to 31, as said below
Outputs:
- fem_image: float32 [32, 8, 4096], P('px', 'py')
- bem_image: float32 [32, 8, 256], P('px', 'py')
Inputs may be any that keep to these rules, and one draw needn't show every extreme that they name: `face_nodes`: the 1024 entries of one partition are distinct. `panel_count`: some owner has all 512 slots live. `round_owner`: distinct rows. `panel_normal`: unit vectors.
All inputs are finite; a program needn't handle non-finite values.
Results may differ from a plain program's by a relative error of at most 0.0001.
Values sent between devices are 32-bit elements; how exact they have to be, the bound alone decides.
A program may use at most 64 MiB of HBM per device.

v0:
```python
import math

import jax
import jax.numpy as jnp
from jax import lax
from jax.sharding import PartitionSpec as P

ROUNDS = 8


SMOOTH_SQ = 0.01
FOUR_PI = 4.0 * math.pi


def padded(block, sides, width):
    for axis, dim in sides:
        count = lax.axis_size(axis)
        forward = [(i, i + 1) for i in range(count - 1)]
        backward = [(target, source) for source, target in forward]
        low = lax.ppermute(
            lax.slice_in_dim(block, block.shape[dim] - width, None, axis=dim), axis, forward
        )
        high = lax.ppermute(lax.slice_in_dim(block, 0, width, axis=dim), axis, backward)
        block = jnp.concatenate([low, block, high], axis=dim)
    return block


def broadcast(block, axis, owner):
    block = jnp.where(lax.axis_index(axis) == owner, block, jnp.zeros_like(block))
    return lax.psum(block, axis)


def block_potential(target_pos, source_weighted, source_pos, source_normal):
    offset = target_pos[:, :, None] - source_pos[:, None, :]
    dist_sq = jnp.sum(offset * offset, axis=0)
    smoothed = dist_sq + SMOOTH_SQ
    normal_dot = jnp.sum(source_normal[:, None, :] * offset, axis=0)
    contrib = normal_dot * source_weighted[None, :] / (FOUR_PI * smoothed * jnp.sqrt(smoothed))
    return jnp.sum(contrib, axis=1)


def per_device(
    nodal_field,
    element_matrix,
    connectivity,
    face_nodes,
    panel_node,
    panel_weight,
    centroid,
    panel_normal,
    panel_count,
    target_index,
    round_owner,
):
    nodal = nodal_field[0, 0]
    connect = connectivity[0, 0]
    matrices = element_matrix[0, 0].reshape(4, 4, -1)
    values = nodal[connect]
    element_out = jnp.sum(matrices * values[None, :, :], axis=1)
    partial_image = jnp.zeros_like(nodal).at[connect.reshape(-1)].add(element_out.reshape(-1))
    face_ids = face_nodes[0, 0]
    outgoing = partial_image[face_ids]
    along_rows = padded(outgoing[0:2], (("px", 0),), 1)
    along_cols = padded(outgoing[2:4], (("py", 0),), 1)
    received = jnp.stack([along_rows[0], along_rows[3], along_cols[0], along_cols[3]])
    fem_image = partial_image.at[face_ids.reshape(-1)].add(received.reshape(-1))
    trace = nodal[panel_node[0, 0]]
    targets = target_index[0, 0]
    target_pos = centroid[0, 0][:, targets]
    target_trace = trace[targets]
    column = lax.axis_index("py")
    slots = trace.shape[0]
    all_slots = jnp.arange(slots, dtype=jnp.int32)
    block_len = min(1024, slots)
    raw_rows = jnp.concatenate(
        [panel_weight[0, 0][None, :], centroid[0, 0], panel_normal[0, 0]], axis=0
    )
    potential = jnp.zeros((targets.shape[0],), jnp.float32)
    for round_no in range(ROUNDS):
        owner_row = round_owner[round_no]
        live_count = panel_count[owner_row, column]
        source_trace, arrived = (
            broadcast(trace, "px", owner_row),
            broadcast(raw_rows, "px", owner_row),
        )
        source_weighted = jnp.where(
            all_slots < live_count, arrived[0] * source_trace, jnp.float32(0.0)
        )
        source_geometry = arrived[1:7]
        piece_pos = source_geometry[0:3, 0:block_len]
        piece_normal = source_geometry[3:6, 0:block_len]
        addition = block_potential(target_pos, source_weighted, piece_pos, piece_normal)
        potential = potential + addition
    bem_image = potential - 0.5 * target_trace
    return (fem_image[None, None], bem_image[None, None])


def solution(mesh):
    return jax.shard_map(
        per_device,
        mesh=mesh,
        in_specs=(
            P("px", "py", None),
            P("px", "py", None, None),
            P("px", "py", None, None),
            P("px", "py", None, None),
            P("px", "py", None),
            P("px", "py", None),
            P("px", "py", None, None),
            P("px", "py", None, None),
            P(),
            P("px", "py", None),
            P(),
        ),
        out_specs=(P("px", "py", None), P("px", "py", None)),
        check_vma=False,
    )
```

profile of v0, /device:TPU:1, one launch (start us, length us, event | category | flops | bytes accessed | tf_op | source)
XLA Modules:
  0.0 1041.9 jit_solution(17572150934146660682)
XLA Ops:
  7.2 1.0 fusion.24
  8.3 1.2 copy.59
  9.6 362.7 %gather_fusion = f32[65536]{0:T(1024)S(1)} fusion(f32[4096]{0:T(1024)S(1)} %bitcast.72, s32[65536]{0:T(1024)S(1)} %broadcast_clamp_fusion), kind=kCustom, calls=%fused_computation | custom fusion | bytes 786432 | tf_op jit(solution)/shard_map/gather | solution.py:58
  372.7 0.8 copy-done.2
  373.9 0.7 multiply_reduce_fusion
  374.6 341.5 %scatter_custom_fusion = f32[4096]{0:T(1024)S(1)} fusion(s32[65536]{0:T(1024)S(1)} %bitcast.80, f32[65536]{0:T(1024)S(1)} %bitcast.81, f32[]{:T(128)} %constant.12.clone.1), kind=kCustom, calls=%fused_computation.73 | custom fusion | flops 65536 | bytes 16388 | tf_op jit(solution)/shard_map/scatter-add | solution.py:60
  716.2 6.2 gather_fusion.1
  722.4 9.6 collective-permute-start.2
  732.0 4.0 collective-permute-start
  736.0 1.9 collective-permute-start.1
  738.0 1.3 collective-permute-start.3
  739.4 3.1 gather_fusion.3
  760.6 1.9 gather_fusion.4
  769.2 6.2 scatter_fusion
  775.4 237.4 %all-reduce.3.cloned.1.call-done = (f32[7,512]{1,0:T(8,128)}, f32[7,512]{1,0:T(8,128)}, f32[7,512]{1,0:T(8,128)}, f32[7,512]{1,0:T(8,128)}, f32[7,512]{1,0:T(8,1...) async-done(((f32[7,512]{1,0:T(8,128)}, f32[7,512]{1,0:T(8,128)}, ...) | async-done | bytes 131088 | tf_op jit(solution)/shard_map/psum | solution.py:30
  1014.3 0.8 fusion.34
  1016.5 0.8 fusion.32
  1018.8 0.8 fusion.30
  1021.0 0.8 fusion.28
  1021.8 2.0 multiply_select_fusion.6
  1023.8 3.8 fusion.2
  1028.3 1.2 multiply_select_fusion
  1030.3 1.2 multiply_select_fusion.2
  1032.2 1.3 multiply_select_fusion.4
  (84 shorter events, 14.6 us)
Async XLA Ops:
  7.2 2.4 copy-start
  7.2 2.3 copy-start.4
  7.2 1005.6 %all-reduce.3.cloned.1.call-start = ((), (), s32[]{:S(2)}) async-start(), calls=%async_computation | async-start | bytes 294912 | tf_op jit(solution)/shard_map/psum | solution.py:30
  372.3 1.2 copy-start.2
  716.2 23.1 %copy-start.9 = (s32[1,1,512]{2,1,0:T(1,128)S(1)}, s32[1,1,512]{2,1,0:T(1,128)}, u32[]{:S(2)}) copy-start(s32[1,1,512]{2,1,0:T(1,128)} %param.15) | copy-start | bytes 6148
  722.4 46.8 %collective-permute-start.2 = (f32[1,256]{1,0:T(1,128)S(1)}, f32[1,256]{1,0:T(1,128)S(1)}, u32[]{:S(2)}, u32[]{:S(2)}) collective-permute-start(f32[1,256]{1,0:T(1,128)S(1)} %bitcast.105), channel_id=1, source_target_pairs={{0,1},{1,2},{2,3},{3,4},{4,5},{5,6},{6,7},{8,9},{9,10},{10,11},{11... | collective-permute-start | bytes 3080 | tf_op jit(solution)/shard_map/ppermute | solution.py:20
  732.0 37.1 %collective-permute-start = (f32[1,256]{1,0:T(1,128)S(1)}, f32[1,256]{1,0:T(1,128)S(1)}, u32[]{:S(2)}, u32[]{:S(2)}) collective-permute-start(f32[1,256]{1,0:T(1,128)S(1)} %bitcast.104), channel_id=1, source_target_pairs={{0,8},{8,16},{16,24},{24,32},{32,40},{40,48},{48,56},{56,64},{64,7... | collective-permute-start | bytes 3080 | tf_op jit(solution)/shard_map/ppermute | solution.py:20
  736.0 33.1 %collective-permute-start.1 = (f32[1,256]{1,0:T(1,128)S(1)}, f32[1,256]{1,0:T(1,128)S(1)}, u32[]{:S(2)}, u32[]{:S(2)}) collective-permute-start(f32[1,256]{1,0:T(1,128)S(1)} %bitcast.103), channel_id=1, source_target_pairs={{8,0},{16,8},{24,16},{32,24},{40,32},{48,40},{56,48},{64,56},{72,6... | collective-permute-start | bytes 3080 | tf_op jit(solution)/shard_map/ppermute | solution.py:23
  738.0 31.2 %collective-permute-start.3 = (f32[1,256]{1,0:T(1,128)S(1)}, f32[1,256]{1,0:T(1,128)S(1)}, u32[]{:S(2)}, u32[]{:S(2)}) collective-permute-start(f32[1,256]{1,0:T(1,128)S(1)} %bitcast.102), channel_id=1, source_target_pairs={{1,0},{2,1},{3,2},{4,3},{5,4},{6,5},{7,6},{9,8},{10,9},{11,10},{12... | collective-permute-start | bytes 3080 | tf_op jit(solution)/shard_map/ppermute | solution.py:23
  739.3 3.2 copy-start.3
  739.3 8.9 copy-start.6
  739.3 8.9 copy-start.7
  739.3 9.2 copy-start.5
  739.4 11.1 %copy-start.16 = (s32[1,1,256]{2,1,0:T(1,128)S(1)}, s32[1,1,256]{2,1,0:T(1,128)}, u32[]{:S(2)}) copy-start(s32[1,1,256]{2,1,0:T(1,128)} %param.20) | copy-start | bytes 3076
  748.4 20.0 %copy-start.8 = (s32[32,8]{0,1:T(8,128)S(1)}, s32[32,8]{0,1:T(8,128)}, u32[]{:S(2)}) copy-start(s32[32,8]{0,1:T(8,128)} %param.19) | copy-start | bytes 3076
  775.4 252.2 %copy-start.1 = (f32[4096]{0:T(1024)}, f32[4096]{0:T(1024)S(1)}, u32[]{:S(2)}) copy-start(f32[4096]{0:T(1024)S(1)} %scatter_fusion) | copy-start | bytes 49156
  1027.7 0.7 copy-start.14
  1027.7 0.7 copy-start.15
  1029.6 0.7 copy-start.12
  1029.6 0.7 copy-start.13
  1031.5 0.7 copy-start.10
  1031.5 0.7 copy-start.11
Sparse Core Ops, SparseCore 0:
  750.6 262.1 all-reduce.2
where the time goes:
time: 1040 us
  local copies, waits for them, and re-layouts  388 us (37%)
  other arithmetic  365 us (35%)
  waiting for transfers between devices  237 us (23%)
  between operations  34.7 us (3%)
  starting transfers between devices  16.9 us (2%)
    gather x2, local copies, waits for them, and re-layouts, per_device(): values = nodal[connect]  363 us
    scatter-add x1, other arithmetic, per_device(): jnp.zeros_like(nodal).at[connect.reshape(-1)].add(element_out.reshape(-1))  342 us
    psum x1, waiting for transfers between devices, broadcast(): return lax.psum(block, axis)  237 us
  transfers between devices with their start and end apart: 5, of which 1 were waited for; matrix products, arithmetic and copies ran while one was open for 2% of the time, Pallas kernels for 0%

commit v1 on v0

v1 whole, which is shorter than its diff:
```python
import functools
import math

import jax
import jax.numpy as jnp
from jax import lax
from jax.experimental import pallas as pl
from jax.experimental.pallas import tpu as pltpu
from jax.sharding import PartitionSpec as P

F32 = jnp.float32
BF16 = jnp.bfloat16
MESH = pl.DeviceIdType.MESH

GX, GY = 32, 8
ROUNDS = 8
CHIPS = GX // 2
ROWS = 512
HI, LO = 32, 128
PAIRS = 8
STEPS = ROWS // (8 * PAIRS)
SMOOTH_SQ = 0.01
FOUR_PI = 4.0 * math.pi


def lookup(rows, index):
    lo, hi = index & (LO - 1), index >> 7
    total = jnp.zeros(index.shape, F32)
    for r, row in enumerate(rows):
        picked = jnp.take_along_axis(jnp.broadcast_to(row, index.shape), lo, axis=1)
        total = jnp.where(hi == r, picked, total)
    return total


def table(ref):
    return [ref[r : r + 1, :] for r in range(HI)]


def stack(x, count):
    return jnp.concatenate([x] * count, axis=0)


def one_hots(index_rows, value_rows):
    io_hi = lax.broadcasted_iota(jnp.int32, (HI, 128), 0).astype(F32).astype(BF16)
    io_lo = lax.broadcasted_iota(jnp.int32, (LO, 128), 0).astype(F32).astype(BF16)
    zero_hi, zero_lo = jnp.zeros((HI, 128), BF16), jnp.zeros((LO, 128), BF16)
    one_lo = jnp.ones((LO, 128), BF16)
    left, right = [], []
    for index, value in zip(index_rows, value_rows):
        hi = jnp.broadcast_to((index >> 7).astype(F32), (16, 128)).astype(BF16)
        lo = jnp.broadcast_to((index & (LO - 1)).astype(F32), (16, 128)).astype(BF16)
        value = jnp.broadcast_to(value, (16, 128))
        upper = value.astype(BF16)
        lower = (value - upper.astype(F32)).astype(BF16)
        at_hi = stack(hi, HI // 16) == io_hi
        left.append(
            jnp.concatenate(
                [
                    jnp.where(at_hi, stack(upper, HI // 16), zero_hi),
                    jnp.where(at_hi, stack(lower, HI // 16), zero_hi),
                ],
                axis=0,
            )
        )
        right.append(jnp.where(stack(lo, LO // 16) == io_lo, one_lo, zero_lo))
    return jnp.concatenate(left, axis=1), jnp.concatenate(right, axis=1)


def scatter_product(index_rows, value_rows):
    left, right = one_hots(index_rows, value_rows)
    return lax.dot_general(left, right, (((1,), (1,)), ((), ())), preferred_element_type=F32)


def kernel(
    count_ref, owner_ref, nodal_ref, conn_ref, matrix_ref, face_ref, node_ref, weight_ref,
    centroid_ref, normal_ref, target_ref,
    fem_ref, bem_ref,
    block, gathered, value, total, partial, sent, incoming, place, small, potential,
    send_sem, recv_sem, face_send, face_recv,
):
    px, py = lax.axis_index("px"), lax.axis_index("py")
    core = lax.rem(px, 2)
    sibling = px + 1 - 2 * core
    low_x, high_x = lax.rem(px + GX - 1, GX), lax.rem(px + 1, GX)
    low_y, high_y = lax.rem(py + GY - 1, GY), lax.rem(py + 1, GY)
    across = jnp.where(core == 0, low_x, high_x)

    barrier = pltpu.get_barrier_semaphore()

    @pl.loop(1, CHIPS)
    def _(d):
        pl.semaphore_signal(
            barrier, inc=1, device_id=(lax.rem(px + 2 * d, GX), py), device_id_type=MESH
        )

    for device in ((sibling, py), (across, py), (px, low_y), (px, high_y)):
        pl.semaphore_signal(barrier, inc=1, device_id=device, device_id_type=MESH)

    sublane = lax.broadcasted_iota(jnp.int32, (8, 128), 0)
    lane = lax.broadcasted_iota(jnp.int32, (8, 128), 1)

    small[0:4, :] = node_ref[...]
    small[4:8, :] = node_ref[...]
    trace = lookup(table(nodal_ref), small[...])
    live = count_ref[py, px]
    slot = (sublane & 3) * 128 + lane
    weight = jnp.concatenate([weight_ref[...], weight_ref[...]], axis=0)
    weighted = jnp.where(slot < live, weight * trace, 0.0)
    block[0:12, :] = centroid_ref[...]
    block[12:24, :] = normal_ref[...] * stack(weighted[0:4, :], 3)

    pl.semaphore_wait(barrier, CHIPS + 3)

    def to_chip(d, source):
        return pltpu.make_async_remote_copy(
            src_ref=block,
            dst_ref=gathered.at[source],
            send_sem=send_sem.at[d],
            recv_sem=recv_sem.at[source],
            device_id=(lax.rem(px + 2 * d, GX), py),
            device_id_type=MESH,
        )

    def to_sibling(d, source, held):
        return pltpu.make_async_remote_copy(
            src_ref=held,
            dst_ref=gathered.at[source],
            send_sem=send_sem.at[CHIPS + d],
            recv_sem=recv_sem.at[source],
            device_id=(sibling, py),
            device_id_type=MESH,
        )

    @pl.loop(1, CHIPS)
    def _(d):
        to_chip(d, px).start()

    to_sibling(0, px, block).start()
    gathered[px] = block[...]

    for i in range(4):
        small[2 * i : 2 * i + 2, :] = target_ref[...]
    targets = small[...]
    target_trace = lookup([trace[k : k + 1, :] for k in range(2)], targets)
    for c in range(3):
        where = lookup([block[4 * c + k : 4 * c + k + 1, :] for k in range(2)], targets)
        for half in range(2):
            place[c, 128 * half : 128 * half + 128, :] = jnp.broadcast_to(
                where[half : half + 1, :], (128, 128)
            ).T

    total[...] = jnp.zeros_like(total)
    odd, second, fourth = (sublane & 1) == 1, (sublane & 2) == 2, (sublane & 4) == 4

    @pl.loop(0, STEPS)
    def _(step):
        base = step * PAIRS
        index_rows, value_rows = [], []
        for u in range(PAIRS):
            at = pl.multiple_of((base + u) * 8, 8)
            nodes = conn_ref[pl.ds(at, 8), :]
            values = lookup(table(nodal_ref), nodes)
            swapped = pltpu.roll(values, 4, 0)
            folded = []
            for chunk in range(2):
                both = jnp.where(fourth, swapped, values) if chunk == 0 else jnp.where(fourth, values, swapped)
                lanes = pl.ds(pl.multiple_of((base + u) * 256 + 128 * chunk, 128), 128)
                first = matrix_ref[0:8, lanes] * both
                last = matrix_ref[8:16, lanes] * both
                folded.append(
                    jnp.where(second, last + pltpu.roll(last, 2, 0), first + pltpu.roll(first, 6, 0))
                )
            value[8 * u : 8 * u + 8, :] = jnp.where(
                odd, folded[1] + pltpu.roll(folded[1], 1, 0), folded[0] + pltpu.roll(folded[0], 7, 0)
            )
            for chunk in range(2):
                for corner in range(4):
                    index_rows.append(conn_ref[pl.ds(at + 4 * chunk + corner, 1), :])
                    row = 8 * u + (0, 4, 2, 6)[corner] + chunk
                    value_rows.append(value[row : row + 1, :])
        total[...] += scatter_product(index_rows, value_rows)

    partial[...] = total[0:HI, :] + total[HI : 2 * HI, :]

    outgoing = lookup(table(partial), face_ref[...])
    for f in range(4):
        for half in range(2):
            sent[f, half : half + 1, :] = outgoing[4 * half + f : 4 * half + f + 1, :]
    neighbours = ((low_x, py), (high_x, py), (px, low_y), (px, high_y))
    faces = [
        pltpu.make_async_remote_copy(
            src_ref=sent.at[f],
            dst_ref=incoming.at[f ^ 1],
            send_sem=face_send.at[f],
            recv_sem=face_recv.at[f ^ 1],
            device_id=neighbours[f],
            device_id_type=MESH,
        )
        for f in range(4)
    ]
    for face in faces:
        face.start()

    @pl.loop(1, CHIPS)
    def _(d):
        source = lax.rem(px + GX - 2 * d, GX)
        to_chip(d, source).wait_recv()
        to_sibling(d, source, gathered.at[source]).start()

    @pl.loop(0, CHIPS)
    def _(d):
        source = lax.rem(sibling + GX - 2 * d, GX)
        to_sibling(d, source, gathered.at[source]).wait_recv()

    @pl.loop(0, 8)
    def _(part):
        spots = [
            [place[c, pl.ds(pl.multiple_of(32 * part + 8 * g, 8), 8), :] for c in range(3)]
            for g in range(4)
        ]

        def one_round(r, sums):
            owner = owner_ref[r]
            sums = list(sums)
            for k in range(4):
                rows = [
                    jnp.broadcast_to(gathered[owner, 4 * c + k : 4 * c + k + 1, :], (8, 128))
                    for c in range(6)
                ]
                for g in range(4):
                    dx, dy, dz = (spots[g][c] - rows[c] for c in range(3))
                    inverse = lax.rsqrt(dx * dx + dy * dy + dz * dz + SMOOTH_SQ)
                    along = rows[3] * dx + rows[4] * dy + rows[5] * dz
                    sums[g] = sums[g] + along * (inverse * inverse * inverse)
            return tuple(sums)

        sums = lax.fori_loop(0, ROUNDS, one_round, (jnp.zeros((8, 128), F32),) * 4)
        for g in range(4):
            potential[pl.ds(pl.multiple_of(32 * part + 8 * g, 8), 8), :] = sums[g]

    for half in range(2):
        summed = jnp.sum(potential[128 * half : 128 * half + 128, :].T, axis=0, keepdims=True)
        bem_ref[half : half + 1, :] = (
            summed * (1.0 / FOUR_PI) - 0.5 * target_trace[half : half + 1, :]
        )

    for face in faces:
        face.wait_recv()
    present = (px > 0, px < GX - 1, py > 0, py < GY - 1)
    index_rows, value_rows = [], []
    for f in range(4):
        for half in range(2):
            row = 4 * half + f
            index_rows.append(face_ref[row : row + 1, :])
            value_rows.append(jnp.where(present[f], incoming[f, half : half + 1, :], 0.0))
    added = scatter_product(index_rows, value_rows)
    fem_ref[...] = partial[...] + added[0:HI, :] + added[HI : 2 * HI, :]

    for face in faces:
        face.wait_send()

    @pl.loop(1, CHIPS)
    def _(d):
        to_chip(d, px).wait_send()

    @pl.loop(0, CHIPS)
    def _(d):
        to_sibling(d, px, block).wait_send()


def per_device(
    nodal_field, element_matrix, connectivity, face_nodes, panel_node, panel_weight,
    centroid, panel_normal, panel_count, target_index, round_owner,
):
    vmem = pl.BlockSpec(memory_space=pltpu.VMEM)
    smem = pl.BlockSpec(memory_space=pltpu.SMEM)
    connect = connectivity[0, 0].reshape(4, 128, 128).transpose(1, 0, 2).reshape(ROWS, 128)
    fem, bem = pl.pallas_call(
        kernel,
        out_shape=(
            jax.ShapeDtypeStruct((HI, LO), F32),
            jax.ShapeDtypeStruct((2, 128), F32),
        ),
        in_specs=[smem, smem] + [vmem] * 9,
        out_specs=(vmem, vmem),
        scratch_shapes=[
            pltpu.VMEM((24, 128), F32),
            pltpu.VMEM((GX, 24, 128), F32),
            pltpu.VMEM((8 * PAIRS, 128), F32),
            pltpu.VMEM((2 * HI, LO), F32),
            pltpu.VMEM((HI, LO), F32),
            pltpu.VMEM((4, 2, 128), F32),
            pltpu.VMEM((4, 2, 128), F32),
            pltpu.VMEM((3, 256, 128), F32),
            pltpu.VMEM((8, 128), jnp.int32),
            pltpu.VMEM((256, 128), F32),
            pltpu.SemaphoreType.DMA((2 * CHIPS,)),
            pltpu.SemaphoreType.DMA((GX,)),
            pltpu.SemaphoreType.DMA((4,)),
            pltpu.SemaphoreType.DMA((4,)),
        ],
        compiler_params=pltpu.CompilerParams(
            collective_id=0, has_side_effects=True, vmem_limit_bytes=32 * 1024 * 1024
        ),
        name="apply",
    )(
        panel_count.T,
        round_owner,
        nodal_field.reshape(HI, LO),
        connect,
        element_matrix[0, 0],
        face_nodes[0, 0].reshape(4, 2, 128).transpose(1, 0, 2).reshape(8, 128),
        panel_node.reshape(4, 128),
        panel_weight.reshape(4, 128),
        centroid.reshape(12, 128),
        panel_normal.reshape(12, 128),
        target_index.reshape(2, 128),
    )
    return fem.reshape(1, 1, HI * LO), bem.reshape(1, 1, 256)


def solution(mesh):
    split = P("px", "py")
    return jax.shard_map(
        per_device,
        mesh=mesh,
        in_specs=(split,) * 8 + (P(), split, P()),
        out_specs=(split, split),
        check_vma=False,
    )
```

time: 1040 us -> 31.6 us (0.03)
  local copies, waits for them, and re-layouts: 388 us -> 5.41 us
  other arithmetic: 365 us -> 0.06 us
  waiting for transfers between devices: 237 us -> 0 us
  between operations: 34.7 us -> 0.72 us
  Pallas kernels: 0 us -> 25.1 us
  starting transfers between devices: 16.9 us -> 0 us
    gather x7 -> x0, local copies, waits for them, and re-layouts: 375 us -> none  [the longest x2 363 us: per_device(): values = nodal[connect]]
    scatter-add x2 -> x0, other arithmetic: 348 us -> none  [the longest x1 342 us: per_device(): jnp.zeros_like(nodal).at[connect.reshape(-1)].add(element_out.reshape(-1))]
    psum x1 -> x0, waiting for transfers between devices: 237 us -> none  [broadcast(): return lax.psum(block, axis)]
    pallas_call x0 -> x1, Pallas kernels: none -> 25.1 us  [per_device(): pl.pallas_call(kernel, out_shape=(jax.ShapeDtypeStruct((HI, LO), F32), ja...]
    ppermute x4 -> x0, starting transfers between devices: 16.9 us -> none  [the longest x2 13.7 us: padded(): lax.ppermute(lax.slice_in_dim(block, block.shape[dim] - width, None, axis...]
  transfers between devices with their start and end apart: 5 -> 0, of which waited for: 1 -> 0; matrix products, arithmetic and copies ran while one was open for 2% -> 0% of each run, Pallas kernels for 0% -> 0%
where the time goes in v1:
time: 31.6 us; the launch traced here: 31.3 us
  Pallas kernels  25.1 us (79%)
  local copies, waits for them, and re-layouts  5.41 us (17%)
  between operations  0.72 us (2%)
    pallas_call x1, Pallas kernels, per_device(): pl.pallas_call(kernel, out_shape=(jax.ShapeDtypeStruct((HI, LO), F32), ja...  25.1 us
    unnamed x24, local copies, waits for them, and re-layouts  5.39 us

profile of v1, /device:TPU:1, one launch (start us, length us, event | category | flops | bytes accessed | tf_op | source)
XLA Modules:
  0.0 31.3 jit_solution(15887850699467473393)
XLA Ops:
  0.6 0.0 copy-start.9
  0.6 0.7 %copy-done.9 = f32[1,1,3,512]{3,1,2,0:T(1,128)S(1)} copy-done((f32[1,1,3,512]{3,1,2,0:T(1,128)S(1)}, f32[1,1,3,512]{3,1,2,0:T(1,128)}, u32[]{:S(2)}) %copy-start.9) | copy-done | bytes 6168
  1.4 0.0 copy-start.10
  1.4 0.7 %copy-done.10 = f32[1,1,3,512]{3,1,2,0:T(1,128)S(1)} copy-done((f32[1,1,3,512]{3,1,2,0:T(1,128)S(1)}, f32[1,1,3,512]{3,1,2,0:T(1,128)}, u32[]{:S(2)}) %copy-start.10) | copy-done | bytes 6168
  2.0 0.0 copy-start.2
  2.1 0.0 copy-start.3
  2.1 0.0 copy-start.4
  2.1 0.0 copy-start.5
  2.1 0.0 copy-start.6
  2.1 0.0 copy-start.7
  2.1 0.0 copy-start.8
  2.2 0.6 %copy-done.2 = f32[1,1,4096]{2,1,0:T(1,128)S(1)} copy-done((f32[1,1,4096]{2,1,0:T(1,128)S(1)}, f32[1,1,4096]{2,1,0:T(1,128)}, u32[]{:S(2)}) %copy-start.2) | copy-done | bytes 16408
  2.8 0.0 copy-done.3
  2.8 0.0 copy-done.4
  2.8 0.0 copy-done.5
  2.8 0.0 copy-done.6
  2.8 0.0 copy-done.7
  2.8 0.0 copy-done.8
  2.8 0.0 copy-start
  2.8 1.2 %copy-done = f32[1,1,16,16384]{3,2,1,0:T(8,128)S(1)} copy-done((f32[1,1,16,16384]{3,2,1,0:T(8,128)S(1)}, f32[1,1,16,16384]{3,2,1,0:T(8,128)}, u32[]{:S(2)}) %copy-start) | copy-done | bytes 1048600
  4.1 0.9 %copy-done.1 = s32[1,1,4,16384]{3,2,1,0:T(4,128)S(1)} copy-done((s32[1,1,4,16384]{3,2,1,0:T(4,128)S(1)}, s32[1,1,4,16384]{3,2,1,0:T(4,128)}, u32[]{:S(2)}) %copy-start.1) | copy-done | bytes 262168
  5.0 25.1 %apply.1 = (f32[32,128]{1,0:T(8,128)S(1)}, f32[2,128]{1,0:T(2,128)S(1)}) custom-call(s32[8,32]{1,0:T(8,128)S(1)} %bitcast.22, s32[8]{0:T(128)S(1)} %copy-done.8, f32[32,128]{1,0:T(8,128)S(1)} %bitcast.20, s32[512,128]{1,0:T(8,128)S(1)} %bitcast.19, f32[16,16384]{1,0:T(8,128)S(1)} %bitcast.18, s32[8,128]{1,0:T(8,128)S(1)} %bitcast.23, s32[4,128]{1,0:T(4,128)S(1)} %bitcast.24, ...), custom_call_target="tpu_custom_call" | custom-call | tf_op jit(solution)/shard_map/apply/pallas_call | solution.py:278
  30.1 0.6 %copy.17 = f32[1,1,4096]{2,1,0:T(1,128)} copy(f32[1,1,4096]{2,1,0:T(1,128)S(1)} %bitcast.21) | data formatting | bytes 32768
  30.7 0.6 %copy.18 = f32[1,1,256]{2,1,0:T(1,128)} copy(f32[1,1,256]{2,1,0:T(1,128)S(1)} %bitcast.26) | data formatting | bytes 2048
  (5 shorter events, 0.1 us)
Async XLA Ops:
  0.6 0.7 %copy-start.9 = (f32[1,1,3,512]{3,1,2,0:T(1,128)S(1)}, f32[1,1,3,512]{3,1,2,0:T(1,128)}, u32[]{:S(2)}) copy-start(f32[1,1,3,512]{3,1,2,0:T(1,128)} %param.17) | copy-start | bytes 18436
  1.4 0.7 %copy-start.10 = (f32[1,1,3,512]{3,1,2,0:T(1,128)S(1)}, f32[1,1,3,512]{3,1,2,0:T(1,128)}, u32[]{:S(2)}) copy-start(f32[1,1,3,512]{3,1,2,0:T(1,128)} %param.18) | copy-start | bytes 18436
  2.0 0.7 %copy-start.2 = (f32[1,1,4096]{2,1,0:T(1,128)S(1)}, f32[1,1,4096]{2,1,0:T(1,128)}, u32[]{:S(2)}) copy-start(f32[1,1,4096]{2,1,0:T(1,128)} %param.11) | copy-start | bytes 49156
  2.1 0.7 %copy-start.3 = (s32[32,8]{0,1:T(8,128)S(1)}, s32[32,8]{0,1:T(8,128)}, u32[]{:S(2)}) copy-start(s32[32,8]{0,1:T(8,128)} %param.19) | copy-start | bytes 3076
  2.1 0.7 %copy-start.4 = (s32[1,1,4,256]{3,2,1,0:T(4,128)S(1)}, s32[1,1,4,256]{3,2,1,0:T(4,128)}, u32[]{:S(2)}) copy-start(s32[1,1,4,256]{3,2,1,0:T(4,128)} %param.14) | copy-start | bytes 12292
  2.1 0.7 %copy-start.5 = (s32[1,1,512]{2,1,0:T(1,128)S(1)}, s32[1,1,512]{2,1,0:T(1,128)}, u32[]{:S(2)}) copy-start(s32[1,1,512]{2,1,0:T(1,128)} %param.15) | copy-start | bytes 6148
  2.1 0.7 %copy-start.6 = (f32[1,1,512]{2,1,0:T(1,128)S(1)}, f32[1,1,512]{2,1,0:T(1,128)}, u32[]{:S(2)}) copy-start(f32[1,1,512]{2,1,0:T(1,128)} %param.16) | copy-start | bytes 6148
  2.1 0.7 %copy-start.7 = (s32[1,1,256]{2,1,0:T(1,128)S(1)}, s32[1,1,256]{2,1,0:T(1,128)}, u32[]{:S(2)}) copy-start(s32[1,1,256]{2,1,0:T(1,128)} %param.20) | copy-start | bytes 3076
  2.1 0.7 %copy-start.8 = (s32[8]{0:T(128)S(1)}, s32[8]{0:T(128)}, u32[]{:S(2)}) copy-start(s32[8]{0:T(128)} %owner_ref.1) | copy-start | bytes 100
  2.8 1.2 %copy-start = (f32[1,1,16,16384]{3,2,1,0:T(8,128)S(1)}, f32[1,1,16,16384]{3,2,1,0:T(8,128)}, u32[]{:S(2)}) copy-start(f32[1,1,16,16384]{3,2,1,0:T(8,128)} %param.12) | copy-start | bytes 3145732
  4.0 0.9 %copy-start.1 = (s32[1,1,4,16384]{3,2,1,0:T(4,128)S(1)}, s32[1,1,4,16384]{3,2,1,0:T(4,128)}, u32[]{:S(2)}) copy-start(s32[1,1,4,16384]{3,2,1,0:T(4,128)} %param.13) | copy-start | bytes 786436

commit v2 on v1

v2 whole, which is shorter than its diff:
```python
import functools
import math

import jax
import jax.numpy as jnp
from jax import lax
from jax.experimental import pallas as pl
from jax.experimental.pallas import tpu as pltpu
from jax.sharding import PartitionSpec as P

F32 = jnp.float32
BF16 = jnp.bfloat16
MESH = pl.DeviceIdType.MESH

GX, GY = 32, 8
ROUNDS = 8
BINS = 64
ROWS = 512
HI, LO = 32, 128
PAIRS = 32
STEPS = ROWS // (8 * PAIRS)
GROUPS = 8
SMOOTH_SQ = 0.01
FOUR_PI = 4.0 * math.pi


def lookup(rows, index):
    lo, hi = index & (LO - 1), index >> 7
    total = jnp.zeros(index.shape, F32)
    for r, row in enumerate(rows):
        picked = jnp.take_along_axis(jnp.broadcast_to(row, index.shape), lo, axis=1)
        total = jnp.where(hi == r, picked, total)
    return total


def table(ref):
    return [ref[r : r + 1, :] for r in range(HI)]


def stack(x, count):
    return jnp.concatenate([x] * count, axis=0)


def one_hots(index_rows, value_rows):
    bins = lax.broadcasted_iota(jnp.int32, (BINS, 128), 0).astype(F32).astype(BF16)
    zero, one = jnp.zeros((BINS, 128), BF16), jnp.ones((BINS, 128), BF16)
    left, right = [], []
    for index, value in zip(index_rows, value_rows):
        hi = (index >> 7) | ((index & 64) >> 1)
        hi = jnp.broadcast_to(hi.astype(F32), (16, 128)).astype(BF16)
        lo = jnp.broadcast_to((index & 63).astype(F32), (16, 128)).astype(BF16)
        value = jnp.broadcast_to(value, (16, 128))
        upper = value.astype(BF16)
        lower = (value - upper.astype(F32)).astype(BF16)
        at_hi = stack(hi, BINS // 16) == bins
        left.append(
            jnp.concatenate(
                [
                    jnp.where(at_hi, stack(upper, BINS // 16), zero),
                    jnp.where(at_hi, stack(lower, BINS // 16), zero),
                ],
                axis=0,
            )
        )
        right.append(jnp.where(stack(lo, BINS // 16) == bins, one, zero))
    return jnp.concatenate(left, axis=1), jnp.concatenate(right, axis=1)


def scatter_product(index_rows, value_rows):
    left, right = one_hots(index_rows, value_rows)
    return lax.dot_general(left, right, (((1,), (1,)), ((), ())), preferred_element_type=F32)


def as_table(sums):
    bins = sums[0:BINS, :] + sums[BINS : 2 * BINS, :]
    return jnp.concatenate([bins[0:HI, :], bins[HI:BINS, :]], axis=1)


def kernel(
    count_hbm, owner_hbm, nodal_hbm, conn_hbm, matrix_hbm, face_hbm, node_hbm, weight_hbm,
    centroid_hbm, normal_hbm, target_hbm,
    fem_ref, bem_ref,
    count_ref, owner_ref, nodal_ref, conn_ref, matrix_ref, face_ref, node_ref, weight_ref,
    centroid_ref, normal_ref, target_ref,
    halves, gathered, value, total, partial, sent, incoming, spots_out, spots_in, place,
    potential, sums_out, sums_in,
    load_sem, conn_sem, matrix_sem, send_sem, recv_sem, face_send, face_recv, pair_send, pair_recv,
):
    px, py = lax.axis_index("px"), lax.axis_index("py")
    core = px & 1
    sibling = px + 1 - 2 * core
    low_y, high_y = (py + GY - 1) & (GY - 1), (py + 1) & (GY - 1)

    names = ("nodal", "node", "count", "weight", "centroid", "normal", "target", "face", "owner")
    sources = (nodal_hbm, node_hbm, count_hbm, weight_hbm, centroid_hbm, normal_hbm, target_hbm, face_hbm, owner_hbm)
    places = (nodal_ref, node_ref, count_ref, weight_ref, centroid_ref, normal_ref, target_ref, face_ref, owner_ref)
    loads = {
        name: pltpu.make_async_copy(source, where, load_sem.at[i])
        for i, (name, source, where) in enumerate(zip(names, sources, places))
    }

    def conn_load(step):
        rows = pl.ds(pl.multiple_of(step * 8 * PAIRS, 8), 8 * PAIRS)
        return pltpu.make_async_copy(conn_hbm.at[rows], conn_ref.at[rows], conn_sem.at[step])

    def matrix_load(step):
        lanes = pl.ds(pl.multiple_of(step * 256 * PAIRS, 128), 256 * PAIRS)
        return pltpu.make_async_copy(
            matrix_hbm.at[:, lanes], matrix_ref.at[:, lanes], matrix_sem.at[step]
        )

    for name in names:
        loads[name].start()

    @pl.loop(0, STEPS)
    def _(step):
        conn_load(step).start()
        matrix_load(step).start()

    barrier = pltpu.get_barrier_semaphore()

    @pl.loop(1, GX)
    def _(d):
        pl.semaphore_signal(
            barrier, inc=1, device_id=((px + d) & (GX - 1), py), device_id_type=MESH
        )

    for column in (low_y, high_y):
        pl.semaphore_signal(barrier, inc=1, device_id=(px, column), device_id_type=MESH)

    sublane = lax.broadcasted_iota(jnp.int32, (8, 128), 0)
    lane = lax.broadcasted_iota(jnp.int32, (8, 128), 1)

    for name in ("nodal", "node", "count", "weight", "centroid", "normal", "target"):
        loads[name].wait()
    trace = lookup(table(nodal_ref), stack(node_ref[...], 2))
    live = count_ref[py, px]
    slot = (sublane & 3) * 128 + lane
    weighted = jnp.where(slot < live, stack(weight_ref[...], 2) * trace, 0.0)
    for h in range(2):
        for c in range(3):
            halves[h, 2 * c : 2 * c + 2, :] = centroid_ref[c, 2 * h : 2 * h + 2, :]
            halves[h, 6 + 2 * c : 8 + 2 * c, :] = (
                normal_ref[c, 2 * h : 2 * h + 2, :] * weighted[2 * h : 2 * h + 2, :]
            )

    targets = stack(target_ref[...], 4)
    target_trace = lookup([trace[k : k + 1, :] for k in range(2)], targets)
    for c in range(3):
        where = lookup([centroid_ref[c, k : k + 1, :] for k in range(2)], targets)
        spots_out[2 * c : 2 * c + 2, :] = where[0:2, :]

    pl.semaphore_wait(barrier, GX + 1)

    def to_other(d, source):
        target = (px + d) & (GX - 1)
        return pltpu.make_async_remote_copy(
            src_ref=halves.at[target & 1],
            dst_ref=gathered.at[source],
            send_sem=send_sem.at[d],
            recv_sem=recv_sem.at[source],
            device_id=(target, py),
            device_id_type=MESH,
        )

    def to_sibling(source, where, n):
        return pltpu.make_async_remote_copy(
            src_ref=source,
            dst_ref=where,
            send_sem=pair_send.at[n],
            recv_sem=pair_recv.at[n],
            device_id=(sibling, py),
            device_id_type=MESH,
        )

    send_spots = to_sibling(spots_out, spots_in, 0)
    send_sums = to_sibling(sums_out, sums_in, 1)

    @pl.loop(1, GX)
    def _(d):
        to_other(d, px).start()

    send_spots.start()
    gathered[px] = halves[core]

    def spread(ref, first):
        for c in range(3):
            for half in range(2):
                row = ref[2 * c + half : 2 * c + half + 1, :]
                rows = slice(first + 128 * half, first + 128 * half + 128)
                place[c, rows, :] = jnp.broadcast_to(row, (128, 128)).T

    total[...] = jnp.zeros_like(total)
    odd, second, fourth = (sublane & 1) == 1, (sublane & 2) == 2, (sublane & 4) == 4

    @pl.loop(0, STEPS)
    def _(step):
        conn_load(step).wait()
        matrix_load(step).wait()
        base = step * PAIRS
        index_rows, value_rows = [], []
        for u in range(PAIRS):
            at = pl.multiple_of((base + u) * 8, 8)
            nodes = conn_ref[pl.ds(at, 8), :]
            values = lookup(table(nodal_ref), nodes)
            swapped = pltpu.roll(values, 4, 0)
            folded = []
            for chunk in range(2):
                pair = (swapped, values) if chunk == 0 else (values, swapped)
                both = jnp.where(fourth, *pair)
                lanes = pl.ds(pl.multiple_of((base + u) * 256 + 128 * chunk, 128), 128)
                first = matrix_ref[0:8, lanes] * both
                last = matrix_ref[8:16, lanes] * both
                folded.append(
                    jnp.where(second, last + pltpu.roll(last, 2, 0), first + pltpu.roll(first, 6, 0))
                )
            value[8 * u : 8 * u + 8, :] = jnp.where(
                odd, folded[1] + pltpu.roll(folded[1], 1, 0), folded[0] + pltpu.roll(folded[0], 7, 0)
            )
            for chunk in range(2):
                for corner in range(4):
                    index_rows.append(conn_ref[pl.ds(at + 4 * chunk + corner, 1), :])
                    row = 8 * u + (0, 4, 2, 6)[corner] + chunk
                    value_rows.append(value[row : row + 1, :])
        total[...] += scatter_product(index_rows, value_rows)

    partial[...] = as_table(total[...])

    loads["face"].wait()
    outgoing = lookup(table(partial), face_ref[...])
    for f in range(4):
        for half in range(2):
            sent[f, half : half + 1, :] = outgoing[4 * half + f : 4 * half + f + 1, :]
    neighbours = (
        ((px + GX - 1) & (GX - 1), py),
        ((px + 1) & (GX - 1), py),
        (px, low_y),
        (px, high_y),
    )
    faces = [
        pltpu.make_async_remote_copy(
            src_ref=sent.at[f],
            dst_ref=incoming.at[f ^ 1],
            send_sem=face_send.at[f],
            recv_sem=face_recv.at[f ^ 1],
            device_id=neighbours[f],
            device_id_type=MESH,
        )
        for f in range(4)
    ]
    for face in faces:
        face.start()

    loads["owner"].wait()
    spread(spots_out, 256)
    send_spots.wait_recv()
    spread(spots_in, 0)

    @pl.loop(1, GX)
    def _(d):
        to_other(d, (px + GX - d) & (GX - 1)).wait_recv()

    def double_layer(first):
        @pl.loop(0, 32 // GROUPS)
        def _(part):
            at = [pl.multiple_of(8 * (GROUPS * part + g), 8) for g in range(GROUPS)]
            spots = [[place[c, pl.ds(first + at[g], 8), :] for c in range(3)] for g in range(GROUPS)]

            def one_round(r, sums):
                owner = owner_ref[r]
                sums = list(sums)
                for k in range(2):
                    rows = [
                        jnp.broadcast_to(gathered[owner, 2 * c + k : 2 * c + k + 1, :], (8, 128))
                        for c in range(6)
                    ]
                    for g in range(GROUPS):
                        dx, dy, dz = (spots[g][c] - rows[c] for c in range(3))
                        inverse = lax.rsqrt(dx * dx + dy * dy + dz * dz + SMOOTH_SQ)
                        along = rows[3] * dx + rows[4] * dy + rows[5] * dz
                        sums[g] = sums[g] + along * (inverse * inverse * inverse)
                return tuple(sums)

            sums = lax.fori_loop(
                0, ROUNDS, one_round, (jnp.zeros((8, 128), F32),) * GROUPS, unroll=2
            )
            for g in range(GROUPS):
                potential[pl.ds(at[g], 8), :] = sums[g]

        return [
            jnp.sum(potential[128 * half : 128 * half + 128, :].T, axis=0, keepdims=True)
            for half in range(2)
        ]

    for half, row in enumerate(double_layer(0)):
        sums_out[half : half + 1, :] = row
    send_sums.start()
    own = double_layer(256)
    send_sums.wait_recv()
    for half in range(2):
        bem_ref[half : half + 1, :] = (
            own[half] + sums_in[half : half + 1, :]
        ) * (1.0 / FOUR_PI) - 0.5 * target_trace[half : half + 1, :]

    send_spots.wait_send()
    send_sums.wait_send()

    @pl.loop(1, GX)
    def _(d):
        to_other(d, px).wait_send()

    for face in faces:
        face.wait_send()
    for face in faces:
        face.wait_recv()
    present = (px > 0, px < GX - 1, py > 0, py < GY - 1)
    index_rows, value_rows = [], []
    for f in range(4):
        for half in range(2):
            row = 4 * half + f
            index_rows.append(face_ref[row : row + 1, :])
            value_rows.append(jnp.where(present[f], incoming[f, half : half + 1, :], 0.0))
    fem_ref[...] = partial[...] + as_table(scatter_product(index_rows, value_rows))


def per_device(
    nodal_field, element_matrix, connectivity, face_nodes, panel_node, panel_weight,
    centroid, panel_normal, panel_count, target_index, round_owner,
):
    vmem = pl.BlockSpec(memory_space=pltpu.VMEM)
    hbm = pl.BlockSpec(memory_space=pl.ANY)
    i32 = jnp.int32
    connect = connectivity[0, 0].reshape(4, 128, 128).transpose(1, 0, 2).reshape(ROWS, 128)
    faces = face_nodes[0, 0].reshape(4, 2, 128).transpose(1, 0, 2).reshape(8, 128)
    fem, bem = pl.pallas_call(
        kernel,
        out_shape=(
            pltpu.VMEM((HI, LO), F32),
            pltpu.VMEM((2, 128), F32),
        ),
        in_specs=[hbm] * 11,
        out_specs=(vmem, vmem),
        scratch_shapes=[
            pltpu.SMEM((GY, GX), i32),
            pltpu.SMEM((ROUNDS,), i32),
            pltpu.VMEM((HI, LO), F32),
            pltpu.VMEM((ROWS, 128), i32),
            pltpu.VMEM((16, ROWS * 32), F32),
            pltpu.VMEM((8, 128), i32),
            pltpu.VMEM((4, 128), i32),
            pltpu.VMEM((4, 128), F32),
            pltpu.VMEM((3, 4, 128), F32),
            pltpu.VMEM((3, 4, 128), F32),
            pltpu.VMEM((2, 128), i32),
            pltpu.VMEM((2, 12, 128), F32),
            pltpu.VMEM((GX, 12, 128), F32),
            pltpu.VMEM((8 * PAIRS, 128), F32),
            pltpu.VMEM((2 * BINS, BINS), F32),
            pltpu.VMEM((HI, LO), F32),
            pltpu.VMEM((4, 2, 128), F32),
            pltpu.VMEM((4, 2, 128), F32),
            pltpu.VMEM((6, 128), F32),
            pltpu.VMEM((6, 128), F32),
            pltpu.VMEM((3, 512, 128), F32),
            pltpu.VMEM((256, 128), F32),
            pltpu.VMEM((2, 128), F32),
            pltpu.VMEM((2, 128), F32),
            pltpu.SemaphoreType.DMA((9,)),
            pltpu.SemaphoreType.DMA((STEPS,)),
            pltpu.SemaphoreType.DMA((STEPS,)),
            pltpu.SemaphoreType.DMA((GX,)),
            pltpu.SemaphoreType.DMA((GX,)),
            pltpu.SemaphoreType.DMA((4,)),
            pltpu.SemaphoreType.DMA((4,)),
            pltpu.SemaphoreType.DMA((2,)),
            pltpu.SemaphoreType.DMA((2,)),
        ],
        compiler_params=pltpu.CompilerParams(
            collective_id=0, has_side_effects=True, vmem_limit_bytes=60 * 1024 * 1024
        ),
        name="apply",
    )(
        panel_count.T,
        round_owner,
        nodal_field.reshape(HI, LO),
        connect,
        element_matrix.reshape(16, -1),
        faces,
        panel_node.reshape(4, 128),
        panel_weight.reshape(4, 128),
        centroid.transpose(0, 2, 1, 3).reshape(3, 4, 128),
        panel_normal.transpose(0, 2, 1, 3).reshape(3, 4, 128),
        target_index.reshape(2, 128),
    )
    return fem.reshape(1, 1, HI * LO), bem.reshape(1, 1, 256)


def solution(mesh):
    split = P("px", "py")
    return jax.shard_map(
        per_device,
        mesh=mesh,
        in_specs=(split,) * 8 + (P(), split, P()),
        out_specs=(split, split),
        check_vma=False,
    )
```

time: 31.6 us -> 24.3 us (0.77)
  local copies, waits for them, and re-layouts: 5.41 us -> 1.17 us
  Pallas kernels: 25.1 us -> 22.4 us
    unnamed x24 -> x2, local copies, waits for them, and re-layouts: 5.39 us -> 1.17 us
    pallas_call x1, Pallas kernels: 25.1 us -> 22.4 us  [per_device(): pl.pallas_call(kernel, out_shape=(pltpu.VMEM((HI, LO), F32), pltpu.VMEM((...]
where the time goes in v2:
time: 24.3 us; the launch traced here: 24.2 us
  Pallas kernels  22.4 us (92%)
  local copies, waits for them, and re-layouts  1.17 us (5%)
  between operations  0.64 us (3%)
    pallas_call x1, Pallas kernels, per_device(): pl.pallas_call(kernel, out_shape=(pltpu.VMEM((HI, LO), F32), pltpu.VMEM((...  22.4 us
    unnamed x2, local copies, waits for them, and re-layouts  1.17 us

profile of v2, /device:TPU:1, one launch (start us, length us, event | category | flops | bytes accessed | tf_op | source)
XLA Modules:
  0.0 24.2 jit_solution(13136783198940752318)
XLA Ops:
  0.6 22.4 %apply.1 = (f32[32,128]{1,0:T(8,128)S(1)}, f32[2,128]{1,0:T(2,128)S(1)}) custom-call(s32[8,32]{1,0:T(8,128)} %bitcast.27, s32[8]{0:T(128)} %owner_hbm.1, f32[32,128]{1,0:T(8,128)} %bitcast.24, s32[512,128]{1,0:T(8,128)} %bitcast.23, f32[16,16384]{1,0:T(8,128)} %bitcast.22, s32[8,128]{1,0:T(8,128)} %bitcast.28, s32[4,128]{1,0:T(4,128)} %bitcast.29, ...), custom_call_target="tpu_custom_call" | custom-call | tf_op jit(solution)/shard_map/apply/pallas_call | solution.py:335
  23.0 0.6 %copy.17 = f32[1,1,4096]{2,1,0:T(1,128)} copy(f32[1,1,4096]{2,1,0:T(1,128)S(1)} %bitcast.20) | data formatting | bytes 32768
  23.6 0.6 %copy.18 = f32[1,1,256]{2,1,0:T(1,128)} copy(f32[1,1,256]{2,1,0:T(1,128)S(1)} %bitcast.21) | data formatting | bytes 2048

commit v3 on v2

--- a/solution.py
+++ b/solution.py
@@ -17,7 +17,7 @@
 BINS = 64
 ROWS = 512
 HI, LO = 32, 128
-PAIRS = 32
+PAIRS = 16
 STEPS = ROWS // (8 * PAIRS)
 GROUPS = 8
 SMOOTH_SQ = 0.01
@@ -84,7 +84,7 @@
     centroid_ref, normal_ref, target_ref,
     halves, gathered, value, total, partial, sent, incoming, spots_out, spots_in, place,
     potential, sums_out, sums_in,
-    load_sem, conn_sem, matrix_sem, send_sem, recv_sem, face_send, face_recv, pair_send, pair_recv,
+    load_sem, conn_sem, matrix_sem, send_sem, recv_sem, face_send, face_recv, pair_send, pair_recv, entered_sem,
 ):
     px, py = lax.axis_index("px"), lax.axis_index("py")
     core = px & 1
@@ -125,76 +125,21 @@
             barrier, inc=1, device_id=((px + d) & (GX - 1), py), device_id_type=MESH
         )
 
-    for column in (low_y, high_y):
-        pl.semaphore_signal(barrier, inc=1, device_id=(px, column), device_id_type=MESH)
+    even = (py & 1) == 0
+
+    @pl.when(even)
+    def _():
+        for column in (low_y, high_y):
+            pl.semaphore_signal(barrier, inc=1, device_id=(px, column), device_id_type=MESH)
 
     sublane = lax.broadcasted_iota(jnp.int32, (8, 128), 0)
     lane = lax.broadcasted_iota(jnp.int32, (8, 128), 1)
 
-    for name in ("nodal", "node", "count", "weight", "centroid", "normal", "target"):
-        loads[name].wait()
-    trace = lookup(table(nodal_ref), stack(node_ref[...], 2))
-    live = count_ref[py, px]
-    slot = (sublane & 3) * 128 + lane
-    weighted = jnp.where(slot < live, stack(weight_ref[...], 2) * trace, 0.0)
-    for h in range(2):
-        for c in range(3):
-            halves[h, 2 * c : 2 * c + 2, :] = centroid_ref[c, 2 * h : 2 * h + 2, :]
-            halves[h, 6 + 2 * c : 8 + 2 * c, :] = (
-                normal_ref[c, 2 * h : 2 * h + 2, :] * weighted[2 * h : 2 * h + 2, :]
-            )
-
-    targets = stack(target_ref[...], 4)
-    target_trace = lookup([trace[k : k + 1, :] for k in range(2)], targets)
-    for c in range(3):
-        where = lookup([centroid_ref[c, k : k + 1, :] for k in range(2)], targets)
-        spots_out[2 * c : 2 * c + 2, :] = where[0:2, :]
-
-    pl.semaphore_wait(barrier, GX + 1)
-
-    def to_other(d, source):
-        target = (px + d) & (GX - 1)
-        return pltpu.make_async_remote_copy(
-            src_ref=halves.at[target & 1],
-            dst_ref=gathered.at[source],
-            send_sem=send_sem.at[d],
-            recv_sem=recv_sem.at[source],
-            device_id=(target, py),
-            device_id_type=MESH,
-        )
-
-    def to_sibling(source, where, n):
-        return pltpu.make_async_remote_copy(
-            src_ref=source,
-            dst_ref=where,
-            send_sem=pair_send.at[n],
-            recv_sem=pair_recv.at[n],
-            device_id=(sibling, py),
-            device_id_type=MESH,
-        )
-
-    send_spots = to_sibling(spots_out, spots_in, 0)
-    send_sums = to_sibling(sums_out, sums_in, 1)
-
-    @pl.loop(1, GX)
-    def _(d):
-        to_other(d, px).start()
-
-    send_spots.start()
-    gathered[px] = halves[core]
-
-    def spread(ref, first):
-        for c in range(3):
-            for half in range(2):
-                row = ref[2 * c + half : 2 * c + half + 1, :]
-                rows = slice(first + 128 * half, first + 128 * half + 128)
-                place[c, rows, :] = jnp.broadcast_to(row, (128, 128)).T
-
+    loads["nodal"].wait()
     total[...] = jnp.zeros_like(total)
     odd, second, fourth = (sublane & 1) == 1, (sublane & 2) == 2, (sublane & 4) == 4
 
-    @pl.loop(0, STEPS)
-    def _(step):
+    def elements(step):
         conn_load(step).wait()
         matrix_load(step).wait()
         base = step * PAIRS
@@ -224,6 +169,74 @@
                     value_rows.append(value[row : row + 1, :])
         total[...] += scatter_product(index_rows, value_rows)
 
+    pl.loop(0, 2)(elements)
+
+    for name in ("node", "count", "weight", "centroid", "normal", "target"):
+        loads[name].wait()
+    trace = lookup(table(nodal_ref), stack(node_ref[...], 2))
+    live = count_ref[py, px]
+    slot = (sublane & 3) * 128 + lane
+    weighted = jnp.where(slot < live, stack(weight_ref[...], 2) * trace, 0.0)
+    for h in range(2):
+        for c in range(3):
+            halves[h, 2 * c : 2 * c + 2, :] = centroid_ref[c, 2 * h : 2 * h + 2, :]
+            halves[h, 6 + 2 * c : 8 + 2 * c, :] = (
+                normal_ref[c, 2 * h : 2 * h + 2, :] * weighted[2 * h : 2 * h + 2, :]
+            )
+
+    targets = stack(target_ref[...], 4)
+    target_trace = lookup([trace[k : k + 1, :] for k in range(2)], targets)
+    for c in range(3):
+        where = lookup([centroid_ref[c, k : k + 1, :] for k in range(2)], targets)
+        spots_out[2 * c : 2 * c + 2, :] = where[0:2, :]
+
+    pl.semaphore_wait(barrier, GX - 1 + 2 * (py & 1))
+
+    @pl.when(jnp.logical_not(even))
+    def _():
+        for column in (low_y, high_y):
+            pl.semaphore_signal(entered_sem, inc=1, device_id=(px, column), device_id_type=MESH)
+
+    def to_other(d, source):
+        target = (px + d) & (GX - 1)
+        return pltpu.make_async_remote_copy(
+            src_ref=halves.at[target & 1],
+            dst_ref=gathered.at[source],
+            send_sem=send_sem.at[d],
+            recv_sem=recv_sem.at[source],
+            device_id=(target, py),
+            device_id_type=MESH,
+        )
+
+    def to_sibling(source, where, n):
+        return pltpu.make_async_remote_copy(
+            src_ref=source,
+            dst_ref=where,
+            send_sem=pair_send.at[n],
+            recv_sem=pair_recv.at[n],
+            device_id=(sibling, py),
+            device_id_type=MESH,
+        )
+
+    send_spots = to_sibling(spots_out, spots_in, 0)
+    send_sums = to_sibling(sums_out, sums_in, 1)
+
+    @pl.loop(1, GX)
+    def _(d):
+        to_other(d, px).start()
+
+    send_spots.start()
+    gathered[px] = halves[core]
+
+    def spread(ref, first):
+        for c in range(3):
+            for half in range(2):
+                row = ref[2 * c + half : 2 * c + half + 1, :]
+                rows = slice(first + 128 * half, first + 128 * half + 128)
+                place[c, rows, :] = jnp.broadcast_to(row, (128, 128)).T
+
+    pl.loop(2, STEPS)(elements)
+
     partial[...] = as_table(total[...])
 
     loads["face"].wait()
@@ -248,7 +261,14 @@
         )
         for f in range(4)
     ]
-    for face in faces:
+    for face in faces[0:2]:
+        face.start()
+
+    @pl.when(even)
+    def _():
+        pl.semaphore_wait(entered_sem, 2)
+
+    for face in faces[2:4]:
         face.start()
 
     loads["owner"].wait()
@@ -374,6 +394,7 @@
             pltpu.SemaphoreType.DMA((4,)),
             pltpu.SemaphoreType.DMA((2,)),
             pltpu.SemaphoreType.DMA((2,)),
+            pltpu.SemaphoreType.REGULAR,
         ],
         compiler_params=pltpu.CompilerParams(
             collective_id=0, has_side_effects=True, vmem_limit_bytes=60 * 1024 * 1024

time: 24.3 us -> 22.3 us (0.918)
  Pallas kernels: 22.4 us -> 20.3 us
    pallas_call x1, Pallas kernels: 22.4 us -> 20.3 us  [per_device(): pl.pallas_call(kernel, out_shape=(pltpu.VMEM((HI, LO), F32), pltpu.VMEM((...]
where the time goes in v3:
time: 22.3 us; the launch traced here: 22.1 us
  Pallas kernels  20.3 us (91%)
  local copies, waits for them, and re-layouts  1.17 us (5%)
  between operations  0.64 us (3%)
    pallas_call x1, Pallas kernels, per_device(): pl.pallas_call(kernel, out_shape=(pltpu.VMEM((HI, LO), F32), pltpu.VMEM((...  20.3 us
    unnamed x2, local copies, waits for them, and re-layouts  1.17 us

profile of v3, /device:TPU:1, one launch (start us, length us, event | category | flops | bytes accessed | tf_op | source)
XLA Modules:
  0.0 22.1 jit_solution(8861765169334806586)
XLA Ops:
  0.6 20.3 %apply.1 = (f32[32,128]{1,0:T(8,128)S(1)}, f32[2,128]{1,0:T(2,128)S(1)}) custom-call(s32[8,32]{1,0:T(8,128)} %bitcast.27, s32[8]{0:T(128)} %owner_hbm.1, f32[32,128]{1,0:T(8,128)} %bitcast.24, s32[512,128]{1,0:T(8,128)} %bitcast.23, f32[16,16384]{1,0:T(8,128)} %bitcast.22, s32[8,128]{1,0:T(8,128)} %bitcast.28, s32[4,128]{1,0:T(4,128)} %bitcast.29, ...), custom_call_target="tpu_custom_call" | custom-call | tf_op jit(solution)/shard_map/apply/pallas_call | solution.py:355
  21.0 0.6 %copy.17 = f32[1,1,4096]{2,1,0:T(1,128)} copy(f32[1,1,4096]{2,1,0:T(1,128)S(1)} %bitcast.20) | data formatting | bytes 32768
  21.6 0.6 %copy.18 = f32[1,1,256]{2,1,0:T(1,128)} copy(f32[1,1,256]{2,1,0:T(1,128)S(1)} %bitcast.21) | data formatting | bytes 2048

commit v4 on v3

--- a/solution.py
+++ b/solution.py
@@ -136,6 +136,25 @@
     lane = lax.broadcasted_iota(jnp.int32, (8, 128), 1)
 
     loads["nodal"].wait()
+    for name in ("node", "count", "weight", "centroid", "normal", "target"):
+        loads[name].wait()
+    trace = lookup(table(nodal_ref), stack(node_ref[...], 2))
+    live = count_ref[py, px]
+    slot = (sublane & 3) * 128 + lane
+    weighted = jnp.where(slot < live, stack(weight_ref[...], 2) * trace, 0.0)
+    for h in range(2):
+        for c in range(3):
+            halves[h, 2 * c : 2 * c + 2, :] = centroid_ref[c, 2 * h : 2 * h + 2, :]
+            halves[h, 6 + 2 * c : 8 + 2 * c, :] = (
+                normal_ref[c, 2 * h : 2 * h + 2, :] * weighted[2 * h : 2 * h + 2, :]
+            )
+
+    targets = stack(target_ref[...], 4)
+    target_trace = lookup([trace[k : k + 1, :] for k in range(2)], targets)
+    for c in range(3):
+        where = lookup([centroid_ref[c, k : k + 1, :] for k in range(2)], targets)
+        spots_out[2 * c : 2 * c + 2, :] = where[0:2, :]
+
     total[...] = jnp.zeros_like(total)
     odd, second, fourth = (sublane & 1) == 1, (sublane & 2) == 2, (sublane & 4) == 4
 
@@ -169,26 +188,8 @@
                     value_rows.append(value[row : row + 1, :])
         total[...] += scatter_product(index_rows, value_rows)
 
-    pl.loop(0, 2)(elements)
-
-    for name in ("node", "count", "weight", "centroid", "normal", "target"):
-        loads[name].wait()
-    trace = lookup(table(nodal_ref), stack(node_ref[...], 2))
-    live = count_ref[py, px]
-    slot = (sublane & 3) * 128 + lane
-    weighted = jnp.where(slot < live, stack(weight_ref[...], 2) * trace, 0.0)
-    for h in range(2):
-        for c in range(3):
-            halves[h, 2 * c : 2 * c + 2, :] = centroid_ref[c, 2 * h : 2 * h + 2, :]
-            halves[h, 6 + 2 * c : 8 + 2 * c, :] = (
-                normal_ref[c, 2 * h : 2 * h + 2, :] * weighted[2 * h : 2 * h + 2, :]
-            )
-
-    targets = stack(target_ref[...], 4)
-    target_trace = lookup([trace[k : k + 1, :] for k in range(2)], targets)
-    for c in range(3):
-        where = lookup([centroid_ref[c, k : k + 1, :] for k in range(2)], targets)
-        spots_out[2 * c : 2 * c + 2, :] = where[0:2, :]
+    ahead = 1 + 2 * (py & 1)
+    pl.loop(0, ahead)(elements)
 
     pl.semaphore_wait(barrier, GX - 1 + 2 * (py & 1))
 
@@ -235,7 +236,7 @@
                 rows = slice(first + 128 * half, first + 128 * half + 128)
                 place[c, rows, :] = jnp.broadcast_to(row, (128, 128)).T
 
-    pl.loop(2, STEPS)(elements)
+    pl.loop(ahead, STEPS)(elements)
 
     partial[...] = as_table(total[...])
 
@@ -264,17 +265,19 @@
     for face in faces[0:2]:
         face.start()
 
-    @pl.when(even)
+    @pl.when(jnp.logical_not(even))
     def _():
-        pl.semaphore_wait(entered_sem, 2)
-
-    for face in faces[2:4]:
-        face.start()
+        for face in faces[2:4]:
+            face.start()
 
     loads["owner"].wait()
     spread(spots_out, 256)
     send_spots.wait_recv()
     spread(spots_in, 0)
+
+    @pl.loop(1, GX)
+    def _(d):
+        to_other(d, px).wait_send()
 
     @pl.loop(1, GX)
     def _(d):
@@ -315,6 +318,13 @@
     for half, row in enumerate(double_layer(0)):
         sums_out[half : half + 1, :] = row
     send_sums.start()
+
+    @pl.when(even)
+    def _():
+        pl.semaphore_wait(entered_sem, 2)
+        for face in faces[2:4]:
+            face.start()
+
     own = double_layer(256)
     send_sums.wait_recv()
     for half in range(2):
@@ -324,10 +334,6 @@
 
     send_spots.wait_send()
     send_sums.wait_send()
-
-    @pl.loop(1, GX)
-    def _(d):
-        to_other(d, px).wait_send()
 
     for face in faces:
         face.wait_send()

time: 22.3 us -> 21.7 us (0.973)
  Pallas kernels: 20.3 us -> 19.7 us
    pallas_call x1, Pallas kernels: 20.3 us -> 19.7 us  [per_device(): pl.pallas_call(kernel, out_shape=(pltpu.VMEM((HI, LO), F32), pltpu.VMEM((...]
where the time goes in v4:
time: 21.7 us; the launch traced here: 21.5 us
  Pallas kernels  19.7 us (91%)
  local copies, waits for them, and re-layouts  1.17 us (5%)
  between operations  0.64 us (3%)
    pallas_call x1, Pallas kernels, per_device(): pl.pallas_call(kernel, out_shape=(pltpu.VMEM((HI, LO), F32), pltpu.VMEM((...  19.7 us
    unnamed x2, local copies, waits for them, and re-layouts  1.17 us

profile of v4, /device:TPU:1, one launch (start us, length us, event | category | flops | bytes accessed | tf_op | source)
XLA Modules:
  0.0 21.5 jit_solution(6553217510662719348)
XLA Ops:
  0.6 19.7 %apply.1 = (f32[32,128]{1,0:T(8,128)S(1)}, f32[2,128]{1,0:T(2,128)S(1)}) custom-call(s32[8,32]{1,0:T(8,128)} %bitcast.27, s32[8]{0:T(128)} %owner_hbm.1, f32[32,128]{1,0:T(8,128)} %bitcast.24, s32[512,128]{1,0:T(8,128)} %bitcast.23, f32[16,16384]{1,0:T(8,128)} %bitcast.22, s32[8,128]{1,0:T(8,128)} %bitcast.28, s32[4,128]{1,0:T(4,128)} %bitcast.29, ...), custom_call_target="tpu_custom_call" | custom-call | tf_op jit(solution)/shard_map/apply/pallas_call | solution.py:361
  20.4 0.6 %copy.17 = f32[1,1,4096]{2,1,0:T(1,128)} copy(f32[1,1,4096]{2,1,0:T(1,128)S(1)} %bitcast.20) | data formatting | bytes 32768
  21.0 0.6 %copy.18 = f32[1,1,256]{2,1,0:T(1,128)} copy(f32[1,1,256]{2,1,0:T(1,128)S(1)} %bitcast.21) | data formatting | bytes 2048

commit v5 on v4

--- a/solution.py
+++ b/solution.py
@@ -126,11 +126,20 @@
         )
 
     even = (py & 1) == 0
-
-    @pl.when(even)
-    def _():
-        for column in (low_y, high_y):
-            pl.semaphore_signal(barrier, inc=1, device_id=(px, column), device_id_type=MESH)
+    late = jnp.logical_not(even)
+    present = (px > 0, px < GX - 1, py > 0, py < GY - 1)
+    columns = present[2].astype(jnp.int32) + present[3].astype(jnp.int32)
+
+    def greet(semaphore, ours):
+        for column, there in ((low_y, present[2]), (high_y, present[3])):
+
+            @pl.when(jnp.logical_and(ours, there))
+            def _():
+                pl.semaphore_signal(
+                    semaphore, inc=1, device_id=(px, column), device_id_type=MESH
+                )
+
+    greet(barrier, even)
 
     sublane = lax.broadcasted_iota(jnp.int32, (8, 128), 0)
     lane = lax.broadcasted_iota(jnp.int32, (8, 128), 1)
@@ -191,12 +200,8 @@
     ahead = 1 + 2 * (py & 1)
     pl.loop(0, ahead)(elements)
 
-    pl.semaphore_wait(barrier, GX - 1 + 2 * (py & 1))
-
-    @pl.when(jnp.logical_not(even))
-    def _():
-        for column in (low_y, high_y):
-            pl.semaphore_signal(entered_sem, inc=1, device_id=(px, column), device_id_type=MESH)
+    pl.semaphore_wait(barrier, GX - 1 + columns * (py & 1))
+    greet(entered_sem, late)
 
     def to_other(d, source):
         target = (px + d) & (GX - 1)
@@ -262,13 +267,10 @@
         )
         for f in range(4)
     ]
-    for face in faces[0:2]:
-        face.start()
-
-    @pl.when(jnp.logical_not(even))
-    def _():
-        for face in faces[2:4]:
-            face.start()
+    for f in range(2):
+        pl.when(present[f])(faces[f].start)
+    for f in range(2, 4):
+        pl.when(jnp.logical_and(late, present[f]))(faces[f].start)
 
     loads["owner"].wait()
     spread(spots_out, 256)
@@ -321,9 +323,10 @@
 
     @pl.when(even)
     def _():
-        pl.semaphore_wait(entered_sem, 2)
-        for face in faces[2:4]:
-            face.start()
+        pl.semaphore_wait(entered_sem, columns)
+
+    for f in range(2, 4):
+        pl.when(jnp.logical_and(even, present[f]))(faces[f].start)
 
     own = double_layer(256)
     send_sums.wait_recv()
@@ -335,17 +338,21 @@
     send_spots.wait_send()
     send_sums.wait_send()
 
-    for face in faces:
-        face.wait_send()
-    for face in faces:
-        face.wait_recv()
-    present = (px > 0, px < GX - 1, py > 0, py < GY - 1)
+    for f in range(4):
+        pl.when(present[f])(faces[f].wait_send)
+    for f in range(4):
+        pl.when(present[f])(faces[f ^ 1].wait_recv)
+
+        @pl.when(jnp.logical_not(present[f]))
+        def _():
+            incoming[f] = jnp.zeros((2, 128), F32)
+
     index_rows, value_rows = [], []
     for f in range(4):
         for half in range(2):
             row = 4 * half + f
             index_rows.append(face_ref[row : row + 1, :])
-            value_rows.append(jnp.where(present[f], incoming[f, half : half + 1, :], 0.0))
+            value_rows.append(incoming[f, half : half + 1, :])
     fem_ref[...] = partial[...] + as_table(scatter_product(index_rows, value_rows))
 
 

time: 21.7 us -> 20.7 us (0.954)
  the two profiles are of different devices: /device:TPU:1 before, /device:TPU:225 now
where the time goes in v5:
time: 20.7 us; the launch traced here: 20.5 us
  Pallas kernels  18.7 us (90%)
  local copies, waits for them, and re-layouts  1.17 us (6%)
  between operations  0.64 us (3%)
    pallas_call x1, Pallas kernels, per_device(): pl.pallas_call(kernel, out_shape=(pltpu.VMEM((HI, LO), F32), pltpu.VMEM((...  18.7 us
    unnamed x2, local copies, waits for them, and re-layouts  1.17 us

profile of v5, /device:TPU:225, one launch (start us, length us, event | category | flops | bytes accessed | tf_op | source)
XLA Modules:
  0.0 20.5 jit_solution(3590173418260330808)
XLA Ops:
  0.6 18.7 %apply.1 = (f32[32,128]{1,0:T(8,128)S(1)}, f32[2,128]{1,0:T(2,128)S(1)}) custom-call(s32[8,32]{1,0:T(8,128)} %bitcast.27, s32[8]{0:T(128)} %owner_hbm.1, f32[32,128]{1,0:T(8,128)} %bitcast.24, s32[512,128]{1,0:T(8,128)} %bitcast.23, f32[16,16384]{1,0:T(8,128)} %bitcast.22, s32[8,128]{1,0:T(8,128)} %bitcast.28, s32[4,128]{1,0:T(4,128)} %bitcast.29, ...), custom_call_target="tpu_custom_call" | custom-call | tf_op jit(solution)/shard_map/apply/pallas_call | solution.py:368
  19.4 0.6 %copy.17 = f32[1,1,4096]{2,1,0:T(1,128)} copy(f32[1,1,4096]{2,1,0:T(1,128)S(1)} %bitcast.20) | data formatting | bytes 32768
  20.0 0.6 %copy.18 = f32[1,1,256]{2,1,0:T(1,128)} copy(f32[1,1,256]{2,1,0:T(1,128)S(1)} %bitcast.21) | data formatting | bytes 2048

commit v6 on v5

--- a/solution.py
+++ b/solution.py
@@ -17,7 +17,7 @@
 BINS = 64
 ROWS = 512
 HI, LO = 32, 128
-PAIRS = 16
+PAIRS = 32
 STEPS = ROWS // (8 * PAIRS)
 GROUPS = 8
 SMOOTH_SQ = 0.01
@@ -197,7 +197,7 @@
                     value_rows.append(value[row : row + 1, :])
         total[...] += scatter_product(index_rows, value_rows)
 
-    ahead = 1 + 2 * (py & 1)
+    ahead = 1
     pl.loop(0, ahead)(elements)
 
     pl.semaphore_wait(barrier, GX - 1 + columns * (py & 1))

time: 20.7 us -> 20.5 us (level)
  the two profiles are of different devices: /device:TPU:225 before, /device:TPU:1 now
where the time goes in v6:
time: 20.5 us; the launch traced here: 20.4 us
  Pallas kernels  18.6 us (91%)
  local copies, waits for them, and re-layouts  1.17 us (6%)
  between operations  0.64 us (3%)
    pallas_call x1, Pallas kernels, per_device(): pl.pallas_call(kernel, out_shape=(pltpu.VMEM((HI, LO), F32), pltpu.VMEM((...  18.6 us
    unnamed x2, local copies, waits for them, and re-layouts  1.17 us

profile of v6, /device:TPU:1, one launch (start us, length us, event | category | flops | bytes accessed | tf_op | source)
XLA Modules:
  0.0 20.4 jit_solution(12379871049872011061)
XLA Ops:
  0.6 18.6 %apply.1 = (f32[32,128]{1,0:T(8,128)S(1)}, f32[2,128]{1,0:T(2,128)S(1)}) custom-call(s32[8,32]{1,0:T(8,128)} %bitcast.27, s32[8]{0:T(128)} %owner_hbm.1, f32[32,128]{1,0:T(8,128)} %bitcast.24, s32[512,128]{1,0:T(8,128)} %bitcast.23, f32[16,16384]{1,0:T(8,128)} %bitcast.22, s32[8,128]{1,0:T(8,128)} %bitcast.28, s32[4,128]{1,0:T(4,128)} %bitcast.29, ...), custom_call_target="tpu_custom_call" | custom-call | tf_op jit(solution)/shard_map/apply/pallas_call | solution.py:368
  19.2 0.6 %copy.17 = f32[1,1,4096]{2,1,0:T(1,128)} copy(f32[1,1,4096]{2,1,0:T(1,128)S(1)} %bitcast.20) | data formatting | bytes 32768
  19.8 0.6 %copy.18 = f32[1,1,256]{2,1,0:T(1,128)} copy(f32[1,1,256]{2,1,0:T(1,128)S(1)} %bitcast.21) | data formatting | bytes 2048
